TPU v7x, 128 devices: a whole 4x4x4 slice. The times are simulated.
128 devices in a mesh: row: 32 (over y_lo, z, x), col: 4 (over y_hi, core).
Axes of the slice: x: 4, y: 4 (y_hi: 2, y_lo: 2; y = y_hi * 2 + y_lo), z: 4, core: 2. Of those that a mesh axis runs over, the one named last changes fastest.
Arguments:
- image: bfloat16 [18432, 1152], P(('row', 'col')), may hold values from -6 to 6
- text: bfloat16 [18432, 1152], P(('col', 'row')), may hold values from -6 to 6
- log_scale: float32 [], replicated, may hold values from 0.9 to 1.3
Outputs:
- loss_value: float32 [], replicated
- image_grad: float32 [18432, 1152], P(('row', 'col'))
- text_grad: float32 [18432, 1152], P(('col', 'row'))
All inputs are finite; a program needn't handle non-finite values.
Results may differ from a plain program's by a relative error of at most 0.00175.
Values may be sent and summed in bfloat16 or wider, within the bound.
No kernel may reach another device: no remote copies, remote signals or barrier semaphores. Data moves between devices by JAX's collectives and lax.ppermute only.
A program may use at most 128 MiB of HBM per device.

v0:
```python
import jax
import jax.numpy as jnp
from jax import lax
from jax.sharding import PartitionSpec as P


def on_device(image, text, log_scale):
    inverse_temp = jnp.exp(log_scale)
    own_rows = image.shape[0]
    image_block = lax.all_gather(image, "col", axis=0, tiled=True)
    text_block = lax.all_gather(text, "row", axis=0, tiled=True)
    scores = inverse_temp * lax.dot_general(
        image_block, text_block, (((1,), (1,)), ((), ())), preferred_element_type=jnp.float32
    )
    block_rows = scores.shape[0]
    block_cols = scores.shape[1]
    row_place = lax.axis_index("row")
    col_place = lax.axis_index("col")
    row_count = lax.axis_size("row")
    row_local = jnp.max(scores, axis=1)
    col_local = jnp.max(scores, axis=0)
    row_top = lax.pmax(row_local, "col")
    col_top = lax.pmax(col_local, "row")
    row_total = lax.psum(jnp.sum(jnp.exp(scores - row_top[:, None]), axis=1), "col")
    col_total = lax.psum(jnp.sum(jnp.exp(scores - col_top[None, :]), axis=0), "row")
    row_lse = row_top + jnp.log(row_total)
    col_lse = col_top + jnp.log(col_total)
    row_global = row_place * block_rows + lax.iota(jnp.int32, block_rows)
    col_global = col_place * block_cols + lax.iota(jnp.int32, block_cols)
    matches = row_global[:, None] == col_global[None, :]
    diagonal_sum = jnp.sum(jnp.where(matches, scores, jnp.float32(0.0)))
    own_row_lse = lax.dynamic_slice_in_dim(row_lse, col_place * own_rows, own_rows)
    own_col_lse = lax.dynamic_slice_in_dim(col_lse, row_place * own_rows, own_rows)
    local_loss = jnp.sum(own_row_lse) + jnp.sum(own_col_lse) - 2.0 * diagonal_sum
    total_rows = block_rows * row_count
    loss_value = lax.psum(local_loss, ("row", "col")) / (2.0 * total_rows)
    weights = (
        0.5 * (jnp.exp(scores - row_lse[:, None]) + jnp.exp(scores - col_lse[None, :]))
        - matches.astype(jnp.float32)
    ).astype(jnp.bfloat16)
    image_term = inverse_temp * jnp.dot(weights, text_block, preferred_element_type=jnp.float32)
    summed_image = lax.psum(image_term, "col")
    image_grad = lax.dynamic_slice_in_dim(summed_image, col_place * own_rows, own_rows, 0)
    text_term = inverse_temp * lax.dot_general(
        weights, image_block, (((0,), (0,)), ((), ())), preferred_element_type=jnp.float32
    )
    text_grad = lax.psum_scatter(text_term, "row", scatter_dimension=0, tiled=True)
    return (loss_value, image_grad, text_grad)


def solution(mesh):
    in_specs = (P(("row", "col"), None), P(("col", "row"), None), P())
    out_specs = (P(), P(("row", "col"), None), P(("col", "row"), None))
    return jax.shard_map(
        on_device, mesh=mesh, in_specs=in_specs, out_specs=out_specs, check_vma=False
    )
```

profile of v0, /device:TPU:0, one launch (start us, length us, event | category | flops | bytes accessed | tf_op | source)
XLA Modules:
  0.0 880.5 jit_solution(574469755010779238)
XLA Ops:
  7.2 0.0 all-gather.3.cloned.1.call-start
  7.2 0.7 all-gather.3.cloned.1.call-update
  7.9 0.0 all-gather.5.cloned.1.call-start
  7.9 0.7 all-gather.5.cloned.1.call-update
  8.6 0.0 all-reduce.2.cloned.1.call-start
  9.4 25.1 %all-gather.3.cloned.1.call-done = bf16[576,1152]{1,0:T(8,128)(2,1)} async-done(((bf16[144,1152]{1,0:T(8,128)(2,1)}), bf16[576,1152]{1,0:T(8,128)(2,1)}) %all-gather.3.cloned.1.call-update) | async-done | bytes 1327120 | tf_op jit(solution)/shard_map/all_gather | solution.py:10
  34.5 173.6 %all-gather.5.cloned.1.call-done = bf16[4608,1152]{1,0:T(8,128)(2,1)} async-done(((bf16[144,1152]{1,0:T(8,128)(2,1)}), bf16[4608,1152]{1,0:T(8,128)(2,1)}) %all-gather.5.cloned.1.call-update) | async-done | bytes 10616848 | tf_op jit(solution)/shard_map/all_gather | solution.py:11
  208.1 12.7 %fusion.5 = (f32[4608]{0:T(1024)S(1)}, f32[576]{0:T(1024)S(1)}, f32[576,4608]{1,0:T(8,128)}) fusion(bf16[576,1152]{1,0:T(8,128)(2,1)} %all-gather.3.cloned.1.call-done, bf16[4608,1152]{1,0:T(8,128)(2,1)} %all-gather.5.cloned.1.call-done, f32[]{:T(128)S(6)} %exp.15), kind=kOutput, calls=%fused_computation.17 | convolution fusion | flops 6123252736 | bytes 22581508 | tf_op jit(solution)/shard_map/dot_general | solution.py:12
  220.8 156.1 %pmax.15 = f32[4608]{0:T(1024)S(1)} all-reduce(f32[4608]{0:T(1024)S(1)} %get-tuple-element.6), channel_id=1, replica_groups=mesh['row'=32,'col'=4] {'row'}, use_global_device_ids=true, to_apply=%region_6.0 | all-reduce | flops 4608 | bytes 36864 | tf_op jit(solution)/shard_map/pmax | solution.py:23
  376.9 7.1 pmax.14
  384.0 8.5 fusion
  392.5 152.1 %psum.29 = f32[4608]{0:T(1024)S(1)} all-reduce(f32[4608]{0:T(1024)S(1)} %get-tuple-element.4), channel_id=1, replica_groups=mesh['row'=32,'col'=4] {'row'}, use_global_device_ids=true, to_apply=%region_8.9 | all-reduce | flops 4608 | bytes 36864 | tf_op jit(solution)/shard_map/psum | solution.py:25
  544.5 7.2 psum.28
  551.7 16.8 %convolution_multiply_fusion.2 = f32[576,1152]{1,0:T(8,128)} fusion(bf16[4608,1152]{1,0:T(8,128)(2,1)} %all-gather.5.cloned.1.call-done, f32[]{:T(128)S(6)} %exp.15, f32[576,4608]{1,0:T(8,128)} %get-tuple-element.8, f32[4608]{0:T(1024)S(1)} %log_add_fusion, f32[576]{0:T(1024)S(1)} %log_add_fusion.1, s32[4608]{0:T(1024)S(1)} %iota_add_fusion, ...), kind=kOutput, calls=%fused_computation.9 | convolution fusion | flops 6137192448 | bytes 23929348 | tf_op jit(solution)/shard_map/dot_general | solution.py:41
  568.5 0.0 all-reduce.2.cloned.1.call-update
  568.5 0.2 reduce-scatter.2.cloned.1.call-start
  568.8 17.8 %convolution_multiply_fusion = f32[4608,1152]{1,0:T(8,128)} fusion(bf16[576,1152]{1,0:T(8,128)(2,1)S(1)} %copy-done, f32[]{:T(128)S(6)} %exp.15, f32[576,4608]{1,0:T(8,128)} %get-tuple-element.8, f32[4608]{0:T(1024)S(1)} %log_add_fusion, f32[576]{0:T(1024)S(1)} %log_add_fusion.1, s32[4608]{0:T(1024)S(1)} %iota_add_fusion, s32[576]{0:T(1024)S(1)} %iota_add_fusion.1), kind=kOutput, calls=%fused_computation | convolution fusion | flops 6141837312 | bytes 33219076 | tf_op jit(solution)/shard_map/dot_general | solution.py:44
  586.6 0.0 reduce-scatter.2.cloned.1.call-update
  586.6 0.8 dynamic-slice_reduce_fusion
  587.4 0.7 dynamic-slice_reduce_fusion.1
  590.0 73.7 %psum.30 = f32[]{:T(128)} all-reduce(f32[]{:T(128)S(6)} %sub.42), channel_id=1, replica_groups=mesh['row'=32,'col'=4] {'row','col'}, use_global_device_ids=true, to_apply=%region_11.12 | all-reduce | flops 1 | bytes 8 | tf_op jit(solution)/shard_map/psum | solution.py:36
  664.4 0.0 all-reduce.2.cloned.1.call-done
  664.4 2.0 constant_dynamic-slice_fusion
  666.4 206.4 %reduce-scatter.2.cloned.1.call-done = f32[144,1152]{1,0:T(8,128)} async-done(((f32[4608,1152]{1,0:T(8,128)}), f32[144,1152]{1,0:T(8,128)}) %reduce-scatter.2.cloned.1.call-update) | async-done | bytes 663568 | tf_op jit(solution)/shard_map/reduce_scatter | solution.py:47
  (6 shorter events, 0.0 us)
Async XLA Ops:
  7.2 27.3 %all-gather.3.cloned.1.call-start = ((), (), s32[]{:S(2)}) async-start(), calls=%async_computation.1 | async-start | bytes 1658880 | tf_op jit(solution)/shard_map/all_gather | solution.py:10
  7.9 200.2 %all-gather.5.cloned.1.call-start = ((), (), s32[]{:S(2)}) async-start(), calls=%async_computation.2 | async-start | bytes 10948608 | tf_op jit(solution)/shard_map/all_gather | solution.py:11
  8.6 655.7 %all-reduce.2.cloned.1.call-start = ((), (), s32[]{:S(2)}) async-start(), calls=%async_computation.3 | async-start | bytes 5308416 | tf_op jit(solution)/shard_map/psum | solution.py:42
  551.7 17.0 %copy-start = (bf16[576,1152]{1,0:T(8,128)(2,1)S(1)}, bf16[576,1152]{1,0:T(8,128)(2,1)}, u32[]{:S(2)}) copy-start(bf16[576,1152]{1,0:T(8,128)(2,1)} %all-gather.3.cloned.1.call-done) | copy-start | bytes 3981316
  568.5 304.3 %reduce-scatter.2.cloned.1.call-start = ((), (), s32[]{:S(2)}) async-start(), calls=%async_computation.4 | async-start | bytes 21897216 | tf_op jit(solution)/shard_map/reduce_scatter | solution.py:47
Sparse Core Ops, SparseCore 0:
  9.7 24.7 all-gather.2
  36.1 171.8 all-gather.4
  568.6 64.7 all-reduce.1
  636.3 236.5 reduce-scatter.1
where the time goes:
time: 882 us; the launch traced here: 880 us
  waiting for transfers between devices  407 us (46%)
  blocking collectives  396 us (45%)
  matrix products  47.3 us (5%)
  between operations  18.3 us (2%)
  other arithmetic  9.93 us (1%)
    reduce_scatter x1, waiting for transfers between devices, on_device(): lax.psum_scatter(text_term, 'row', scatter_dimension=0, tiled=True)  206 us
    all_gather x1, waiting for transfers between devices, on_device(): text_block = lax.all_gather(text, 'row', axis=0, tiled=True)  174 us
    pmax x1, blocking collectives, on_device(): col_top = lax.pmax(col_local, 'row')  156 us
    psum x1, blocking collectives, on_device(): lax.psum(jnp.sum(jnp.exp(scores - col_top[None, :]), axis=0), 'row')  152 us
    psum x1, blocking collectives, on_device(): loss_value = lax.psum(local_loss, ('row', 'col')) / (2.0 * total_rows)  73.7 us
    all_gather x1, waiting for transfers between devices, on_device(): image_block = lax.all_gather(image, 'col', axis=0, tiled=True)  25.1 us
    dot_general x1, matrix products, on_device(): lax.dot_general(weights, image_block, (((0,), (0,)), ((), ())), preferred...  17.8 us
  transfers between devices with their start and end apart: 4, of which 3 were waited for; matrix products, arithmetic and copies ran while one was open for 2% of the time, Pallas kernels for 0%

commit v1 on v0

v1 whole, which is shorter than its diff:
```python
import jax
import jax.numpy as jnp
from jax import lax
from jax.sharding import Mesh, PartitionSpec as P

AXES = ("ylo", "z", "x", "yhi", "core")
RING = 4


def ring_shift(value, axis, step):
    return lax.ppermute(value, axis, [(i, (i + step) % RING) for i in range(RING)])


def swap(value, axis):
    return lax.ppermute(value, axis, [(0, 1), (1, 0)])


def merge(pairs):
    top = pairs[0][0]
    for pair in pairs[1:]:
        top = jnp.maximum(top, pair[0])
    total = sum(pair[1] * jnp.exp(pair[0] - top) for pair in pairs)
    return jnp.stack([top, total])


def ring_merge(stat, axis):
    pairs = [stat]
    for step in range(1, RING):
        pairs.append(jnp.roll(ring_shift(stat, axis, step), step, axis=1))
    return merge(pairs)


def on_device(image, text, log_scale):
    inverse_temp = jnp.exp(log_scale)
    rows, width = image.shape
    place = {a: lax.axis_index(a) for a in AXES}

    text_far = swap(text, "ylo")
    image_far = swap(image, "yhi")
    text_slots = {(0, 0): text, (0, 1): text_far}
    image_slots = {(0, 0): image, (0, 1): image_far}
    for h in range(2):
        for step in (1, 3, 2):
            text_slots[step, h] = ring_shift(text_slots[0, h], "z", step)
            image_slots[step, h] = ring_shift(image_slots[0, h], "x", step)
    image_near = jnp.concatenate([image_slots[d, h] for h in range(2) for d in range(RING)])
    image_block = jnp.concatenate([image_near, swap(image_near, "core")])
    text_block = jnp.concatenate([text_slots[d, h] for h in range(2) for d in range(RING)])

    back = jnp.arange(RING, dtype=jnp.int32)
    pair = jnp.arange(2, dtype=jnp.int32)
    x_of = (place["x"] - back) % RING
    z_of = (place["z"] - back) % RING
    yhi_of = place["yhi"] ^ pair
    ylo_of = place["ylo"] ^ pair
    core_of = place["core"] ^ pair
    image_ids = (((place["ylo"] * 4 + place["z"]) * 4 + x_of[None, None, :]) * 4
                 + yhi_of[None, :, None] * 2 + core_of[:, None, None]).reshape(-1)
    text_ids = ((place["yhi"] * 2 + place["core"]) * 32
                + (ylo_of[:, None] * 4 + z_of[None, :]) * 4 + place["x"]).reshape(-1)
    within = jnp.arange(rows, dtype=jnp.int32)
    row_ids = (image_ids[:, None] * rows + within).reshape(-1)
    col_ids = (text_ids[:, None] * rows + within).reshape(-1)

    scores = inverse_temp * lax.dot_general(
        image_block, text_block, (((1,), (1,)), ((), ())), preferred_element_type=jnp.float32
    )
    row_top = jnp.max(scores, axis=1)
    col_top = jnp.max(scores, axis=0)
    row_total = jnp.sum(jnp.exp(scores - row_top[:, None]), axis=1)
    col_total = jnp.sum(jnp.exp(scores - col_top[None, :]), axis=0)
    matches = row_ids[:, None] == col_ids[None, :]
    diagonal_sum = jnp.sum(jnp.where(matches, scores, jnp.float32(0.0)))

    row_stat = jnp.stack([row_top, row_total]).reshape(2, 2, 2, RING, rows).transpose(0, 3, 1, 2, 4)
    col_stat = jnp.stack([col_top, col_total]).reshape(2, 2, RING, rows).transpose(0, 2, 1, 3)
    row_stat = ring_merge(row_stat, "x")
    col_stat = ring_merge(col_stat, "z")
    row_stat = merge([row_stat, swap(row_stat, "yhi")[:, :, :, ::-1]])
    col_stat = merge([col_stat, swap(col_stat, "ylo")[:, :, ::-1]])
    row_stat = merge([row_stat, swap(row_stat, "core")[:, :, ::-1]])
    row_lse = (row_stat[0] + jnp.log(row_stat[1])).transpose(1, 2, 0, 3).reshape(-1)
    col_lse = (col_stat[0] + jnp.log(col_stat[1])).transpose(1, 0, 2).reshape(-1)

    total_rows = rows * 128
    local_loss = jnp.sum(row_lse[:rows]) + jnp.sum(col_lse[:rows]) - 2.0 * diagonal_sum
    loss_value = lax.psum(local_loss, AXES) / (2.0 * total_rows)

    weights = (
        0.5 * (jnp.exp(scores - row_lse[:, None]) + jnp.exp(scores - col_lse[None, :]))
        - matches.astype(jnp.float32)
    ).astype(jnp.bfloat16)

    half = RING * rows

    def image_part(lo):
        return jnp.dot(weights[lo:lo + half], text_block, preferred_element_type=jnp.float32)

    def text_part(lo):
        return lax.dot_general(
            weights[:, lo:lo + half], image_block, (((0,), (0,)), ((), ())), preferred_element_type=jnp.float32
        )

    def ring_sum(part, axis):
        part16 = part.astype(jnp.float16)
        total = part[:rows]
        for step in range(1, RING):
            total = total + ring_shift(part16[step * rows:(step + 1) * rows], axis, -step).astype(jnp.float32)
        return total

    text_far_sum = ring_sum(text_part(half), "z")
    image_other = [image_part(2 * half + half * h).astype(jnp.float16) for h in (1, 0)]
    image_far_part = image_part(half) + swap(image_other[0], "core").astype(jnp.float32)
    image_far_sum = ring_sum(image_far_part, "x")
    image_near_part = image_part(0) + swap(image_other[1], "core").astype(jnp.float32)
    image_grad = ring_sum(image_near_part, "x") + swap(image_far_sum.astype(jnp.float16), "yhi").astype(jnp.float32)
    text_grad = ring_sum(text_part(0), "z") + swap(text_far_sum.astype(jnp.float16), "ylo").astype(jnp.float32)
    return loss_value, inverse_temp * image_grad, inverse_temp * text_grad


def solution(mesh):
    fine = Mesh(mesh.devices.reshape(2, 4, 4, 2, 2), AXES)
    in_specs = (P(AXES, None), P(("yhi", "core", "ylo", "z", "x"), None), P())
    out_specs = (P(), P(AXES, None), P(("yhi", "core", "ylo", "z", "x"), None))
    return jax.shard_map(
        on_device, mesh=fine, in_specs=in_specs, out_specs=out_specs, check_vma=False
    )
```

time: 882 us -> 287 us (0.33)
  waiting for transfers between devices: 407 us -> 75.3 us
  blocking collectives: 396 us -> 64.7 us
  starting transfers between devices: 0.34 us -> 48.3 us
  local copies, waits for them, and re-layouts: 2 us -> 22.8 us
  other arithmetic: 9.93 us -> 22.7 us
  between operations: 18.3 us -> 5.85 us
    reduce_scatter x1 -> x0, waiting for transfers between devices: 206 us -> none  [on_device(): lax.psum_scatter(text_term, 'row', scatter_dimension=0, tiled=True)]
    all_gather x2 -> x0, waiting for transfers between devices: 199 us -> none  [the longest x1 174 us: on_device(): text_block = lax.all_gather(text, 'row', axis=0, tiled=True)]
    psum x3 -> x1, blocking collectives: 233 us -> 64.7 us  [on_device(): loss_value = lax.psum(local_loss, AXES) / (2.0 * total_rows)]
    pmax x2 -> x0, blocking collectives: 163 us -> none  [the longest x1 156 us: on_device(): col_top = lax.pmax(col_local, 'row')]
    ppermute x0 -> x40, waiting for transfers between devices: none -> 75.3 us  [the longest x30 69.2 us: ring_shift(): lax.ppermute(value, axis, [(i, (i + step) % RING) for i in range(RING)])]
    ppermute x0 -> x40, starting transfers between devices: none -> 48.3 us  [the longest x30 37.8 us: ring_shift(): lax.ppermute(value, axis, [(i, (i + step) % RING) for i in range(RING)])]
    unnamed x2 -> x30, local copies, waits for them, and re-layouts: 0.01 us -> 17.3 us
    convert_element_type x0 -> x3, other arithmetic: none -> 8.9 us  [the longest x1 7.4 us: on_device(): weights = (0.5 * (jnp.exp(scores - row_lse[:, None]) + jnp.exp(scores - c...]
  transfers between devices with their start and end apart: 4 -> 40, of which waited for: 3 -> 16; matrix products, arithmetic and copies ran while one was open for 2% -> 11% of each run, Pallas kernels for 0% -> 0%
where the time goes in v1:
time: 287 us; the launch traced here: 282 us
  waiting for transfers between devices  75.3 us (26%)
  blocking collectives  64.7 us (23%)
  starting transfers between devices  48.3 us (17%)
  matrix products  42 us (15%)
  local copies, waits for them, and re-layouts  22.8 us (8%)
  other arithmetic  22.7 us (8%)
  between operations  5.85 us (2%)
    ppermute x30, waiting for transfers between devices, ring_shift(): lax.ppermute(value, axis, [(i, (i + step) % RING) for i in range(RING)])  69.2 us
    psum x1, blocking collectives, on_device(): loss_value = lax.psum(local_loss, AXES) / (2.0 * total_rows)  64.7 us
    ppermute x30, starting transfers between devices, ring_shift(): lax.ppermute(value, axis, [(i, (i + step) % RING) for i in range(RING)])  37.8 us
    unnamed x30, local copies, waits for them, and re-layouts  17.3 us
    dot_general x4, matrix products, image_part(): jnp.dot(weights[lo:lo + half], text_block, preferred_element_type=jnp.flo...  16.1 us
    dot_general x2, matrix products, text_part(): lax.dot_general(weights[:, lo:lo + half], image_block, (((0,), (0,)), (()...  13.6 us
    dot_general x1, matrix products, on_device(): lax.dot_general(image_block, text_block, (((1,), (1,)), ((), ())), prefer...  12.4 us
    ppermute x10, starting transfers between devices, swap(): return lax.ppermute(value, axis, [(0, 1), (1, 0)])  10.6 us
  transfers between devices with their start and end apart: 40, of which 16 were waited for; matrix products, arithmetic and copies ran while one was open for 11% of the time, Pallas kernels for 0%

profile of v1, /device:TPU:0, one launch (start us, length us, event | category | flops | bytes accessed | tf_op | source)
XLA Modules:
  0.0 281.8 jit_solution(5529744322366290250)
XLA Ops:
  0.6 2.9 %collective-permute-start.2 = (bf16[144,1152]{1,0:T(8,128)(2,1)}, bf16[144,1152]{1,0:T(8,128)(2,1)S(1)}, u32[]{:S(2)}, u32[]{:S(2)}) collective-permute-start(bf16[144,1152]{1,0:T(8,128)(2,1)} %param.3), channel_id=1, source_target_pairs={{0,12},{4,0},{8,4},{12,8},{1,13},{5,1},{9,5},{13,9},{2,14},{6,2},{... | collective-permute-start | bytes 995336 | tf_op jit(solution)/shard_map/ppermute | solution.py:11
  5.2 3.2 %collective-permute-start.3 = (bf16[144,1152]{1,0:T(8,128)(2,1)}, bf16[144,1152]{1,0:T(8,128)(2,1)S(1)}, u32[]{:S(2)}, u32[]{:S(2)}) collective-permute-start(bf16[144,1152]{1,0:T(8,128)(2,1)} %param.3), channel_id=1, source_target_pairs={{0,2},{2,0},{1,3},{3,1},{4,6},{6,4},{5,7},{7,5},{8,10},{10,8},{9,1... | collective-permute-start | bytes 995336 | tf_op jit(solution)/shard_map/ppermute | solution.py:15
  8.4 4.0 %collective-permute-start.10 = (bf16[144,1152]{1,0:T(8,128)(2,1)}, bf16[144,1152]{1,0:T(8,128)(2,1)S(1)}, u32[]{:S(2)}, u32[]{:S(2)}) collective-permute-start(bf16[144,1152]{1,0:T(8,128)(2,1)} %param.4), channel_id=1, source_target_pairs={{0,48},{16,0},{32,16},{48,32},{1,49},{17,1},{33,17},{49,33},{2,50}... | collective-permute-start | bytes 995336 | tf_op jit(solution)/shard_map/ppermute | solution.py:11
  14.5 7.1 %collective-permute-done = bf16[144,1152]{1,0:T(8,128)(2,1)S(1)} collective-permute-done((bf16[144,1152]{1,0:T(8,128)(2,1)}, bf16[144,1152]{1,0:T(8,128)(2,1)S(1)}, u32[]{:S(2)}, u32[]{:S(2)}) %collective-permute-start) | collective-permute-done | bytes 331808 | tf_op jit(solution)/shard_map/ppermute | solution.py:11
  21.6 3.9 %collective-permute-start.9 = (bf16[144,1152]{1,0:T(8,128)(2,1)}, bf16[144,1152]{1,0:T(8,128)(2,1)}, u32[]{:S(2)}, u32[]{:S(2)}) collective-permute-start(bf16[144,1152]{1,0:T(8,128)(2,1)} %param.4), channel_id=1, source_target_pairs={{0,32},{16,48},{32,0},{48,16},{1,33},{17,49},{33,1},{49,17},{2,34}... | collective-permute-start | bytes 995336 | tf_op jit(solution)/shard_map/ppermute | solution.py:11
  31.1 14.0 %collective-permute-done.4 = bf16[144,1152]{1,0:T(8,128)(2,1)S(1)} collective-permute-done((bf16[144,1152]{1,0:T(8,128)(2,1)S(1)}, bf16[144,1152]{1,0:T(8,128)(2,1)S(1)}, u32[]{:S(2)}, u32[]{:S(2)}) %collective-permute-start.4) | collective-permute-done | bytes 331808 | tf_op jit(solution)/shard_map/ppermute | solution.py:11
  48.9 6.0 %collective-permute-done.6 = bf16[144,1152]{1,0:T(8,128)(2,1)S(1)} collective-permute-done((bf16[144,1152]{1,0:T(8,128)(2,1)S(1)}, bf16[144,1152]{1,0:T(8,128)(2,1)S(1)}, u32[]{:S(2)}, u32[]{:S(2)}) %collective-permute-start.6) | collective-permute-done | bytes 331808 | tf_op jit(solution)/shard_map/ppermute | solution.py:11
  68.5 10.4 %collective-permute-done.12 = bf16[144,1152]{1,0:T(8,128)(2,1)S(1)} collective-permute-done((bf16[144,1152]{1,0:T(8,128)(2,1)}, bf16[144,1152]{1,0:T(8,128)(2,1)S(1)}, u32[]{:S(2)}, u32[]{:S(2)}) %collective-permute-start.12) | collective-permute-done | bytes 331808 | tf_op jit(solution)/shard_map/ppermute | solution.py:11
  83.9 12.4 %fusion.72 = (f32[1152]{0:T(1024)S(1)}, f32[2304]{0:T(1024)S(1)}, f32[2304,1152]{1,0:T(8,128)}) fusion(bf16[2304,1152]{1,0:T(8,128)(2,1)} %constant_dynamic-update-slice_fusion.8, bf16[1152,1152]{1,0:T(8,128)(2,1)S(1)} %copy-done.2, f32[]{:T(128)S(6)} %exp.91), kind=kOutput, calls=%fused_computation.184 | convolution fusion | flops 6123254784 | bytes 18593284 | tf_op jit(solution)/shard_map/dot_general | solution.py:65
  96.5 9.1 %fusion = (f32[]{:T(128)}, f32[1152]{0:T(1024)S(1)}, f32[2304]{0:T(1024)S(1)}) fusion(f32[2304,1152]{1,0:T(8,128)} %get-tuple-element.50, s32[1152]{0:T(1024)S(1)} %add.316, s32[2304]{0:T(1024)S(1)} %add.302, f32[1152]{0:T(1024)S(1)} %get-tuple-element.6, f32[2304]{0:T(1024)S(1)} %get-tuple-element.7), kind=kLoop, calls=%fused_computation.3 | loop fusion | flops 18576000 | bytes 10658308 | tf_op jit(solution)/shard_map/reduce_sum | solution.py:73
  116.8 3.3 %collective-permute-start.18 = (f32[2,4,2,2,144]{4,1,3,2,0:T(4,128)S(1)}, f32[2,4,2,2,144]{4,1,3,2,0:T(4,128)S(1)}, u32[]{:S(2)}, u32[]{:S(2)}) collective-permute-start(f32[2,4,2,2,144]{4,1,3,2,0:T(4,128)S(1)} %pad_maximum_fusion), channel_id=1, source_target_pairs={{0,2},{2,0},{1,3},{3,1},{4,6},{6,4},{5,7},{7,5},{8,10},{10,8},{9,1... | collective-permute-start | bytes 55304 | tf_op jit(solution)/shard_map/ppermute | solution.py:15
  123.9 7.4 %fusion.2 = bf16[2304,1152]{1,0:T(8,128)(2,1)S(1)} fusion(f32[2304,1152]{1,0:T(8,128)} %get-tuple-element.50, f32[1152]{0:T(1024)S(1)} %reshape.178, f32[2304]{0:T(1024)S(1)} %reshape.177, s32[1152]{0:T(1024)S(1)} %add.316, s32[2304]{0:T(1024)S(1)} %add.302), kind=kLoop, calls=%fused_computation.5 | loop fusion | flops 21233664 | bytes 15952896 | tf_op jit(solution)/shard_map/convert_element_type | solution.py:92
  132.0 3.1 %convolution_convert_fusion = f16[576,1152]{1,0:T(8,128)(2,1)} fusion(bf16[1152,1152]{1,0:T(8,128)(2,1)S(1)} %copy-done.3, bf16[2304,1152]{1,0:T(8,128)(2,1)S(1)} %fusion.2), kind=kOutput, calls=%fused_computation.10 | convolution fusion | flops 1529487360 | bytes 5308416 | tf_op jit(solution)/shard_map/dot_general | solution.py:97
  135.2 8.3 %fusion.84 = (f16[576,1152]{1,0:T(8,128)(2,1)S(1)}, f32[576,1152]{1,0:T(8,128)}) fusion(bf16[2304,1152]{1,0:T(8,128)(2,1)} %constant_dynamic-update-slice_fusion.8, bf16[2304,1152]{1,0:T(8,128)(2,1)S(1)} %fusion.2), kind=kOutput, calls=%fused_computation.196 | convolution fusion | flops 3058311168 | bytes 12238848 | tf_op jit(solution)/shard_map/dot_general | solution.py:100
  143.5 5.2 %fusion.85 = (f16[576,1152]{1,0:T(8,128)(2,1)S(1)}, f32[576,1152]{1,0:T(8,128)}) fusion(bf16[2304,1152]{1,0:T(8,128)(2,1)S(1)} %bitcast.247, bf16[2304,1152]{1,0:T(8,128)(2,1)S(1)} %fusion.2), kind=kOutput, calls=%fused_computation.197 | convolution fusion | flops 3058311168 | bytes 12238848 | tf_op jit(solution)/shard_map/dot_general | solution.py:100
  150.1 5.3 %convolution_convert_fusion.1 = f16[576,1152]{1,0:T(8,128)(2,1)} fusion(bf16[1152,1152]{1,0:T(8,128)(2,1)} %constant_dynamic-update-slice_fusion.17, bf16[2304,1152]{1,0:T(8,128)(2,1)} %copy-done), kind=kOutput, calls=%fused_computation.11 | convolution fusion | flops 1529487360 | bytes 5308416 | tf_op jit(solution)/shard_map/dot_general | solution.py:97
  155.4 64.7 %psum.7 = f32[]{:T(128)} all-reduce(f32[]{:T(128)S(6)} %sub.166), channel_id=1, replica_groups=mesh['ylo'=2,'z'=4,'x'=4,'yhi'=2,'core'=2] {'ylo','z','x','yhi','core'}, use_global_device_ids=true, to_apply=%region_7.8 | all-reduce | flops 1 | bytes 8 | tf_op jit(solution)/shard_map/psum | solution.py:87
  227.1 11.4 %collective-permute-done.36 = f16[144,1152]{1,0:T(8,128)(2,1)S(1)} collective-permute-done((f16[144,1152]{1,0:T(8,128)(2,1)}, f16[144,1152]{1,0:T(8,128)(2,1)S(1)}, u32[]{:S(2)}, u32[]{:S(2)}) %collective-permute-start.36) | collective-permute-done | bytes 331808 | tf_op jit(solution)/shard_map/ppermute | solution.py:11
  238.5 4.0 %collective-permute-start.33 = (f16[144,1152]{1,0:T(8,128)(2,1)S(1)}, f16[144,1152]{1,0:T(8,128)(2,1)S(1)}, u32[]{:S(2)}, u32[]{:S(2)}) collective-permute-start(f16[144,1152]{1,0:T(8,128)(2,1)S(1)} %get-tuple-element.10), channel_id=1, source_target_pairs={{0,48},{16,0},{32,16},{48,32},{1,49},{17,1},{33,17},{49,33},{2,50}... | collective-permute-start | bytes 995336 | tf_op jit(solution)/shard_map/ppermute | solution.py:11
  243.8 3.8 %fusion.82 = (f16[576,1152]{1,0:T(8,128)(2,1)S(1)}, f32[576,1152]{1,0:T(8,128)S(1)}) fusion(f16[576,1152]{1,0:T(8,128)(2,1)} %collective-permute-done.28, bf16[1152,1152]{1,0:T(8,128)(2,1)S(1)} %copy-done.4, bf16[2304,1152]{1,0:T(8,128)(2,1)} %copy-done), kind=kOutput, calls=%fused_computation.194 | convolution fusion | flops 1530814464 | bytes 9289728 | tf_op jit(solution)/shard_map/dot_general | solution.py:97
  251.0 3.8 %fusion.83 = (f16[576,1152]{1,0:T(8,128)(2,1)S(1)}, f32[576,1152]{1,0:T(8,128)S(1)}) fusion(f16[576,1152]{1,0:T(8,128)(2,1)} %collective-permute-done.24, bf16[1152,1152]{1,0:T(8,128)(2,1)S(1)} %copy-done.4, bf16[2304,1152]{1,0:T(8,128)(2,1)} %copy-done), kind=kOutput, calls=%fused_computation.195 | convolution fusion | flops 1530814464 | bytes 9289728 | tf_op jit(solution)/shard_map/dot_general | solution.py:97
  255.0 6.7 %collective-permute-done.29 = f16[144,1152]{1,0:T(8,128)(2,1)S(1)} collective-permute-done((f16[144,1152]{1,0:T(8,128)(2,1)S(1)}, f16[144,1152]{1,0:T(8,128)(2,1)S(1)}, u32[]{:S(2)}, u32[]{:S(2)}) %collective-permute-start.29) | collective-permute-done | bytes 331808 | tf_op jit(solution)/shard_map/ppermute | solution.py:11
  261.6 3.4 %collective-permute-done.31 = f16[144,1152]{1,0:T(8,128)(2,1)S(1)} collective-permute-done((f16[144,1152]{1,0:T(8,128)(2,1)S(1)}, f16[144,1152]{1,0:T(8,128)(2,1)S(1)}, u32[]{:S(2)}, u32[]{:S(2)}) %collective-permute-start.31) | collective-permute-done | bytes 331808 | tf_op jit(solution)/shard_map/ppermute | solution.py:11
  275.3 3.9 %collective-permute-done.27 = f16[144,1152]{1,0:T(8,128)(2,1)S(1)} collective-permute-done((f16[144,1152]{1,0:T(8,128)(2,1)S(1)}, f16[144,1152]{1,0:T(8,128)(2,1)S(1)}, u32[]{:S(2)}, u32[]{:S(2)}) %collective-permute-start.27) | collective-permute-done | bytes 331808 | tf_op jit(solution)/shard_map/ppermute | solution.py:11
  (151 shorter events, 68.6 us)
Async XLA Ops:
  0.6 28.3 %collective-permute-start.2 = (bf16[144,1152]{1,0:T(8,128)(2,1)}, bf16[144,1152]{1,0:T(8,128)(2,1)S(1)}, u32[]{:S(2)}, u32[]{:S(2)}) collective-permute-start(bf16[144,1152]{1,0:T(8,128)(2,1)} %param.3), channel_id=1, source_target_pairs={{0,12},{4,0},{8,4},{12,8},{1,13},{5,1},{9,5},{13,9},{2,14},{6,2},{... | collective-permute-start | bytes 995336 | tf_op jit(solution)/shard_map/ppermute | solution.py:11
  3.5 22.8 %collective-permute-start.1 = (bf16[144,1152]{1,0:T(8,128)(2,1)}, bf16[144,1152]{1,0:T(8,128)(2,1)S(1)}, u32[]{:S(2)}, u32[]{:S(2)}) collective-permute-start(bf16[144,1152]{1,0:T(8,128)(2,1)} %param.3), channel_id=1, source_target_pairs={{0,8},{4,12},{8,0},{12,4},{1,9},{5,13},{9,1},{13,5},{2,10},{6,14},... | collective-permute-start | bytes 995336 | tf_op jit(solution)/shard_map/ppermute | solution.py:11
  4.3 17.3 %collective-permute-start = (bf16[144,1152]{1,0:T(8,128)(2,1)}, bf16[144,1152]{1,0:T(8,128)(2,1)S(1)}, u32[]{:S(2)}, u32[]{:S(2)}) collective-permute-start(bf16[144,1152]{1,0:T(8,128)(2,1)} %param.3), channel_id=1, source_target_pairs={{0,4},{4,8},{8,12},{12,0},{1,5},{5,9},{9,13},{13,1},{2,6},{6,10},{... | collective-permute-start | bytes 995336 | tf_op jit(solution)/shard_map/ppermute | solution.py:11
  5.2 22.1 %collective-permute-start.3 = (bf16[144,1152]{1,0:T(8,128)(2,1)}, bf16[144,1152]{1,0:T(8,128)(2,1)S(1)}, u32[]{:S(2)}, u32[]{:S(2)}) collective-permute-start(bf16[144,1152]{1,0:T(8,128)(2,1)} %param.3), channel_id=1, source_target_pairs={{0,2},{2,0},{1,3},{3,1},{4,6},{6,4},{5,7},{7,5},{8,10},{10,8},{9,1... | collective-permute-start | bytes 995336 | tf_op jit(solution)/shard_map/ppermute | solution.py:15
  8.4 57.6 %collective-permute-start.10 = (bf16[144,1152]{1,0:T(8,128)(2,1)}, bf16[144,1152]{1,0:T(8,128)(2,1)S(1)}, u32[]{:S(2)}, u32[]{:S(2)}) collective-permute-start(bf16[144,1152]{1,0:T(8,128)(2,1)} %param.4), channel_id=1, source_target_pairs={{0,48},{16,0},{32,16},{48,32},{1,49},{17,1},{33,17},{49,33},{2,50}... | collective-permute-start | bytes 995336 | tf_op jit(solution)/shard_map/ppermute | solution.py:11
  21.6 41.7 %collective-permute-start.9 = (bf16[144,1152]{1,0:T(8,128)(2,1)}, bf16[144,1152]{1,0:T(8,128)(2,1)}, u32[]{:S(2)}, u32[]{:S(2)}) collective-permute-start(bf16[144,1152]{1,0:T(8,128)(2,1)} %param.4), channel_id=1, source_target_pairs={{0,32},{16,48},{32,0},{48,16},{1,33},{17,49},{33,1},{49,17},{2,34}... | collective-permute-start | bytes 995336 | tf_op jit(solution)/shard_map/ppermute | solution.py:11
  26.3 35.1 %collective-permute-start.8 = (bf16[144,1152]{1,0:T(8,128)(2,1)}, bf16[144,1152]{1,0:T(8,128)(2,1)}, u32[]{:S(2)}, u32[]{:S(2)}) collective-permute-start(bf16[144,1152]{1,0:T(8,128)(2,1)} %param.4), channel_id=1, source_target_pairs={{0,16},{16,32},{32,48},{48,0},{1,17},{17,33},{33,49},{49,1},{2,18}... | collective-permute-start | bytes 995336 | tf_op jit(solution)/shard_map/ppermute | solution.py:11
  27.3 19.2 %collective-permute-start.5 = (bf16[144,1152]{1,0:T(8,128)(2,1)S(1)}, bf16[144,1152]{1,0:T(8,128)(2,1)S(1)}, u32[]{:S(2)}, u32[]{:S(2)}) collective-permute-start(bf16[144,1152]{1,0:T(8,128)(2,1)S(1)} %collective-permute-done.3), channel_id=1, source_target_pairs={{0,8},{4,12},{8,0},{12,4},{1,9},{5,13},{9,1},{13,5},{2,10},{6,14},... | collective-permute-start | bytes 995336 | tf_op jit(solution)/shard_map/ppermute | solution.py:11
  28.9 16.2 %collective-permute-start.4 = (bf16[144,1152]{1,0:T(8,128)(2,1)S(1)}, bf16[144,1152]{1,0:T(8,128)(2,1)S(1)}, u32[]{:S(2)}, u32[]{:S(2)}) collective-permute-start(bf16[144,1152]{1,0:T(8,128)(2,1)S(1)} %collective-permute-done.3), channel_id=1, source_target_pairs={{0,4},{4,8},{8,12},{12,0},{1,5},{5,9},{9,13},{13,1},{2,6},{6,10},{... | collective-permute-start | bytes 995336 | tf_op jit(solution)/shard_map/ppermute | solution.py:11
  46.5 12.6 %collective-permute-start.11 = (bf16[144,1152]{1,0:T(8,128)(2,1)S(1)}, bf16[144,1152]{1,0:T(8,128)(2,1)}, u32[]{:S(2)}, u32[]{:S(2)}) collective-permute-start(bf16[144,1152]{1,0:T(8,128)(2,1)S(1)} %copy-done.1), channel_id=1, source_target_pairs={{0,64},{64,0},{1,65},{65,1},{2,66},{66,2},{3,67},{67,3},{4,68},{68... | collective-permute-start | bytes 995336 | tf_op jit(solution)/shard_map/ppermute | solution.py:15
  55.6 25.6 %collective-permute-start.7 = (bf16[1152,1152]{1,0:T(8,128)(2,1)}, bf16[1152,1152]{1,0:T(8,128)(2,1)S(1)}, u32[]{:S(2)}, u32[]{:S(2)}) collective-permute-start(bf16[1152,1152]{1,0:T(8,128)(2,1)} %get-tuple-element.22), channel_id=1, source_target_pairs={{0,1},{1,0},{2,3},{3,2},{4,5},{5,4},{6,7},{7,6},{8,9},{9,8},{10,11... | collective-permute-start | bytes 7962632 | tf_op jit(solution)/shard_map/ppermute | solution.py:15
  59.1 21.3 %collective-permute-start.14 = (bf16[144,1152]{1,0:T(8,128)(2,1)}, bf16[144,1152]{1,0:T(8,128)(2,1)S(1)}, u32[]{:S(2)}, u32[]{:S(2)}) collective-permute-start(bf16[144,1152]{1,0:T(8,128)(2,1)} %collective-permute-done.11), channel_id=1, source_target_pairs={{0,48},{16,0},{32,16},{48,32},{1,49},{17,1},{33,17},{49,33},{2,50}... | collective-permute-start | bytes 995336 | tf_op jit(solution)/shard_map/ppermute | solution.py:11
  61.4 18.3 %collective-permute-start.13 = (bf16[144,1152]{1,0:T(8,128)(2,1)}, bf16[144,1152]{1,0:T(8,128)(2,1)S(1)}, u32[]{:S(2)}, u32[]{:S(2)}) collective-permute-start(bf16[144,1152]{1,0:T(8,128)(2,1)} %collective-permute-done.11), channel_id=1, source_target_pairs={{0,32},{16,48},{32,0},{48,16},{1,33},{17,49},{33,1},{49,17},{2,34}... | collective-permute-start | bytes 995336 | tf_op jit(solution)/shard_map/ppermute | solution.py:11
  63.4 15.6 %collective-permute-start.12 = (bf16[144,1152]{1,0:T(8,128)(2,1)}, bf16[144,1152]{1,0:T(8,128)(2,1)S(1)}, u32[]{:S(2)}, u32[]{:S(2)}) collective-permute-start(bf16[144,1152]{1,0:T(8,128)(2,1)} %collective-permute-done.11), channel_id=1, source_target_pairs={{0,16},{16,32},{32,48},{48,0},{1,17},{17,33},{33,49},{49,1},{2,18}... | collective-permute-start | bytes 995336 | tf_op jit(solution)/shard_map/ppermute | solution.py:11
  220.1 29.8 %collective-permute-start.24 = (f16[576,1152]{1,0:T(8,128)(2,1)}, f16[576,1152]{1,0:T(8,128)(2,1)}, u32[]{:S(2)}, u32[]{:S(2)}) collective-permute-start(f16[576,1152]{1,0:T(8,128)(2,1)} %convolution_convert_fusion.1), channel_id=1, source_target_pairs={{0,1},{1,0},{2,3},{3,2},{4,5},{5,4},{6,7},{7,6},{8,9},{9,8},{10,11... | collective-permute-start | bytes 3981320 | tf_op jit(solution)/shard_map/ppermute | solution.py:15
  220.1 23.7 %collective-permute-start.28 = (f16[576,1152]{1,0:T(8,128)(2,1)}, f16[576,1152]{1,0:T(8,128)(2,1)}, u32[]{:S(2)}, u32[]{:S(2)}) collective-permute-start(f16[576,1152]{1,0:T(8,128)(2,1)} %convolution_convert_fusion), channel_id=1, source_target_pairs={{0,1},{1,0},{2,3},{3,2},{4,5},{5,4},{6,7},{7,6},{8,9},{9,8},{10,11... | collective-permute-start | bytes 3981320 | tf_op jit(solution)/shard_map/ppermute | solution.py:15
  221.7 16.8 %collective-permute-start.36 = (f16[144,1152]{1,0:T(8,128)(2,1)}, f16[144,1152]{1,0:T(8,128)(2,1)S(1)}, u32[]{:S(2)}, u32[]{:S(2)}) collective-permute-start(f16[144,1152]{1,0:T(8,128)(2,1)} %get-tuple-element.13), channel_id=1, source_target_pairs={{0,48},{16,0},{32,16},{48,32},{1,49},{17,1},{33,17},{49,33},{2,50}... | collective-permute-start | bytes 995336 | tf_op jit(solution)/shard_map/ppermute | solution.py:11
  223.8 18.7 %collective-permute-start.38 = (f16[144,1152]{1,0:T(8,128)(2,1)S(1)}, f16[144,1152]{1,0:T(8,128)(2,1)S(1)}, u32[]{:S(2)}, u32[]{:S(2)}) collective-permute-start(f16[144,1152]{1,0:T(8,128)(2,1)S(1)} %get-tuple-element.14), channel_id=1, source_target_pairs={{0,16},{16,32},{32,48},{48,0},{1,17},{17,33},{33,49},{49,1},{2,18}... | collective-permute-start | bytes 995336 | tf_op jit(solution)/shard_map/ppermute | solution.py:11
  223.8 18.7 %collective-permute-start.37 = (f16[144,1152]{1,0:T(8,128)(2,1)S(1)}, f16[144,1152]{1,0:T(8,128)(2,1)S(1)}, u32[]{:S(2)}, u32[]{:S(2)}) collective-permute-start(f16[144,1152]{1,0:T(8,128)(2,1)S(1)} %get-tuple-element.15), channel_id=1, source_target_pairs={{0,32},{16,48},{32,0},{48,16},{1,33},{17,49},{33,1},{49,17},{2,34}... | collective-permute-start | bytes 995336 | tf_op jit(solution)/shard_map/ppermute | solution.py:11
  238.5 28.6 %collective-permute-start.33 = (f16[144,1152]{1,0:T(8,128)(2,1)S(1)}, f16[144,1152]{1,0:T(8,128)(2,1)S(1)}, u32[]{:S(2)}, u32[]{:S(2)}) collective-permute-start(f16[144,1152]{1,0:T(8,128)(2,1)S(1)} %get-tuple-element.10), channel_id=1, source_target_pairs={{0,48},{16,0},{32,16},{48,32},{1,49},{17,1},{33,17},{49,33},{2,50}... | collective-permute-start | bytes 995336 | tf_op jit(solution)/shard_map/ppermute | solution.py:11
  242.5 24.9 %collective-permute-start.35 = (f16[144,1152]{1,0:T(8,128)(2,1)S(1)}, f16[144,1152]{1,0:T(8,128)(2,1)S(1)}, u32[]{:S(2)}, u32[]{:S(2)}) collective-permute-start(f16[144,1152]{1,0:T(8,128)(2,1)S(1)} %get-tuple-element.11), channel_id=1, source_target_pairs={{0,16},{16,32},{32,48},{48,0},{1,17},{17,33},{33,49},{49,1},{2,18}... | collective-permute-start | bytes 995336 | tf_op jit(solution)/shard_map/ppermute | solution.py:11
  247.8 13.8 %collective-permute-start.29 = (f16[144,1152]{1,0:T(8,128)(2,1)S(1)}, f16[144,1152]{1,0:T(8,128)(2,1)S(1)}, u32[]{:S(2)}, u32[]{:S(2)}) collective-permute-start(f16[144,1152]{1,0:T(8,128)(2,1)S(1)} %get-tuple-element.19), channel_id=1, source_target_pairs={{0,12},{4,0},{8,4},{12,8},{1,13},{5,1},{9,5},{13,9},{2,14},{6,2},{... | collective-permute-start | bytes 995336 | tf_op jit(solution)/shard_map/ppermute | solution.py:11
  249.4 15.6 %collective-permute-start.31 = (f16[144,1152]{1,0:T(8,128)(2,1)S(1)}, f16[144,1152]{1,0:T(8,128)(2,1)S(1)}, u32[]{:S(2)}, u32[]{:S(2)}) collective-permute-start(f16[144,1152]{1,0:T(8,128)(2,1)S(1)} %get-tuple-element.20), channel_id=1, source_target_pairs={{0,4},{4,8},{8,12},{12,0},{1,5},{5,9},{9,13},{13,1},{2,6},{6,10},{... | collective-permute-start | bytes 995336 | tf_op jit(solution)/shard_map/ppermute | solution.py:11
  249.9 15.1 %collective-permute-start.30 = (f16[144,1152]{1,0:T(8,128)(2,1)S(1)}, f16[144,1152]{1,0:T(8,128)(2,1)S(1)}, u32[]{:S(2)}, u32[]{:S(2)}) collective-permute-start(f16[144,1152]{1,0:T(8,128)(2,1)S(1)} %get-tuple-element.21), channel_id=1, source_target_pairs={{0,8},{4,12},{8,0},{12,4},{1,9},{5,13},{9,1},{13,5},{2,10},{6,14},... | collective-permute-start | bytes 995336 | tf_op jit(solution)/shard_map/ppermute | solution.py:11
  (24 other events, 212.6 us)
